TPU v7x, 32 devices: a whole 2x2x4 slice. The times are simulated.
32 devices in a mesh: aa: 4 (over x, core), ba: 8 (over z, y).
Axes of the slice: x: 2, y: 2, z: 4, core: 2. Of those that a mesh axis runs over, the one named last changes fastest.
Arguments:
- grid_field: float32 [64, 192, 10256], P('aa', 'ba'), may hold values from -6 to 6
- cycle_points: int32 [64], P('aa'), may hold values from 2576 to 10256, as said below
- wave_ids: int32 [32], replicated, may hold values from 0 to 2559, as said below
- legendre: bfloat16 [32, 64, 2560], P('aa', 'ba'), may hold values from -0.75 to 0.75
- diffusion: float32 [192], P('ba'), may hold values from 0.3 to 30
Outputs:
- spectra: bfloat16 [32, 192, 2, 2560], P('aa', 'ba')
- grid_out: float32 [64, 192, 10256], P('aa', 'ba')
Inputs may be any that keep to these rules, and one draw needn't show every extreme that they name: `cycle_points`: each cycle holds 4 i + 16 points for an octahedral cycle number i; cycles are ordered by length, and the longest cycle has 10256 points. `wave_ids`: the wavenumbers are distinct; 0 and 2559 are among them.
All inputs are finite; a program needn't handle non-finite values.
Results may differ from a plain program's by a relative error of at most 0.0051.
Values may be sent and summed in bfloat16 or wider, within the bound.
A program may use at most 384 MiB of HBM per device.

v0:
```python
import math

import jax
import jax.numpy as jnp
from jax import lax
from jax.sharding import PartitionSpec as P

highest = lax.Precision.HIGHEST


def cycle_tables(lengths, waves, points):
    column = jnp.arange(points, dtype=jnp.int32)
    turns = waves[None, :, None] * column[None, None, :] % lengths[:, None, None]
    theta = turns.astype(jnp.float32) * (2.0 * math.pi / lengths.astype(jnp.float32))[:, None, None]
    live = (column[None, None, :] < lengths[:, None, None]) & (
        2 * waves[None, :, None] < lengths[:, None, None]
    )
    cosine = jnp.where(live, jnp.cos(theta), jnp.float32(0.0))
    sine = jnp.where(live, jnp.sin(theta), jnp.float32(0.0))
    return jnp.concatenate([cosine, -sine], axis=1)


def damping_factor(diffusion, cut_off):
    degree = jnp.arange(cut_off, dtype=jnp.int32).astype(jnp.float32)
    ratio = degree * (degree + 1.0) / jnp.float32(cut_off * (cut_off - 1))
    return 1.0 / (1.0 + diffusion[:, None] * (ratio * ratio)[None, :])


def per_device(grid_field, cycle_points, wave_ids, legendre, diffusion):
    groups = lax.axis_size("aa")
    waves_total = wave_ids.shape[0]
    per_group = waves_total // groups
    cycle_count = grid_field.shape[0]
    local_fields = grid_field.shape[1]
    points = grid_field.shape[2]
    cut_off = legendre.shape[2]
    own_waves = lax.dynamic_slice_in_dim(wave_ids, lax.axis_index("aa") * per_group, per_group)
    degree = jnp.arange(cut_off, dtype=jnp.int32)
    keep = degree[None, None, None, :] >= own_waves[:, None, None, None]
    damping = damping_factor(diffusion, cut_off)
    tables = cycle_tables(cycle_points, wave_ids, points)
    coeffs = jnp.einsum("rfp,rjp->rfj", grid_field, tables, precision=highest)
    coeffs = coeffs * lax.rsqrt(cycle_points.astype(jnp.float32))[:, None, None]
    fourier = coeffs.reshape(cycle_count, local_fields, 2, waves_total).astype(jnp.bfloat16)
    by_wave = jnp.transpose(fourier, (3, 0, 1, 2)).reshape(
        waves_total, cycle_count, local_fields * 2
    )
    gathered = lax.all_to_all(by_wave, "aa", split_axis=0, concat_axis=1, tiled=True)
    table_all = lax.all_gather(legendre, "ba", axis=1, tiled=True)
    spectral = jnp.einsum("mrk,mrn->mkn", gathered, table_all, preferred_element_type=jnp.float32)
    spectral = spectral.reshape(per_group, local_fields, 2, cut_off)
    spectra = jnp.where(keep, spectral, jnp.float32(0.0)).astype(jnp.bfloat16)
    damped = (spectra.astype(jnp.float32) * damping[None, :, None, :]).astype(jnp.bfloat16)
    flat = damped.reshape(per_group, local_fields * 2, cut_off)
    returned = jnp.einsum(
        "mrn,mkn->mrk", table_all, flat, preferred_element_type=jnp.float32
    ).astype(jnp.bfloat16)
    by_band = lax.all_to_all(returned, "aa", split_axis=1, concat_axis=0, tiled=True)
    by_cycle = jnp.transpose(by_band, (1, 0, 2))
    weight = jnp.where(wave_ids == 0, 1.0, 2.0).astype(jnp.float32) * lax.rsqrt(
        jnp.float32(waves_total)
    )
    pairs = (
        by_cycle.astype(jnp.float32).reshape(cycle_count, waves_total, local_fields, 2)
        * weight[None, :, None, None]
    )
    stacked = jnp.concatenate([pairs[:, :, :, 0], pairs[:, :, :, 1]], axis=1)
    grid_out = jnp.einsum("rjf,rjp->rfp", stacked, tables, precision=highest)
    return (spectra, grid_out)


def solution(mesh):
    in_specs = (P("aa", "ba", None), P("aa"), P(), P("aa", "ba", None), P("ba"))
    out_specs = (P("aa", "ba", None, None), P("aa", "ba", None))
    return jax.shard_map(
        per_device, mesh=mesh, in_specs=in_specs, out_specs=out_specs, check_vma=False
    )
```

profile of v0, /device:TPU:0, one launch (start us, length us, event | category | flops | bytes accessed | tf_op | source)
XLA Modules:
  0.0 499.0 jit_solution(3028550482493548047)
XLA Ops:
  7.2 0.7 all-gather.2.cloned.1.call-update
  7.9 0.7 broadcast_compare_fusion.1
  8.6 0.7 compare_select_fusion
  9.2 0.7 convert_rsqrt_fusion
  9.9 0.8 iota_compare_fusion
  10.7 0.7 broadcast_multiply_fusion
  11.4 1.0 iota_multiply_fusion
  12.3 1.0 broadcast_compare_fusion
  13.3 379.8 %and_select_fusion.1 = (f32[16,32,10256]{2,1,0:T(8,128)}, f32[16,32,10256]{2,1,0:T(8,128)}) fusion(f32[16]{0:T(128)S(1)} %get-tuple-element.7, s32[16]{0:T(128)S(1)} %compare_select_fusion, s32[32,10256]{1,0:T(8,128)S(1)} %iota_multiply_fusion, pred[16]{0:T(512)(128)(4,1)S(1)} %broadcast_compare_fusion.1, pred[16,32]{1,0:T(8,128)(4,1)S(1)} %broadcast_compare_fusion, ...), kind=kLoop, calls=%fused_computation.8 | loop fusion | flops 68263936 | bytes 43486096 | tf_op jit(solution)/shard_map/jit(_where)/select_n | solution.py:18
  393.2 40.3 %fusion.17 = bf16[16,24,64]{2,1,0:T(8,128)(2,1)S(1)} fusion(f32[16,24,10256]{2,1,0:T(8,128)S(1)} %bitcast.30, f32[16,32,10256]{2,1,0:T(8,128)} %get-tuple-element.3, f32[16,32,10256]{2,1,0:T(8,128)} %get-tuple-element.2, f32[16]{0:T(128)S(1)} %get-tuple-element.6), kind=kOutput, calls=%fused_computation.28 | convolution fusion | flops 3035168768 | bytes 57811008 | tf_op jit(solution)/shard_map/rfp,rjp->rfj/dot_general | solution.py:42
  433.5 0.1 convert_element_type.60
  433.7 0.3 copy.23
  434.0 0.8 reshape.176
  434.8 4.2 all-to-all-start
  439.1 0.1 iota_compare_fusion.1
  439.2 0.1 add_divide_fusion
  439.3 0.2 mul.118
  439.5 0.3 mul.119
  439.8 3.2 all-to-all-done
  443.0 0.2 reshape.177
  443.2 3.7 fusion.27
  447.0 4.1 reshape.165
  451.0 3.2 fusion.16
  454.2 0.1 copy.26
  454.4 0.8 reshape.178
  455.2 3.6 all-to-all-start.1
  458.7 3.1 select_convert_fusion.1
  461.9 0.9 all-to-all-done.1
  462.7 0.2 reshape.179
  463.0 0.2 copy.29
  463.2 0.2 copy_multiply_fusion
  463.5 28.3 %fusion = f32[16,24,10256]{2,1,0:T(8,128)} fusion(f32[16,32,10256]{2,1,0:T(8,128)} %get-tuple-element.3, f32[16,32,10256]{2,1,0:T(8,128)} %get-tuple-element.2, f32[16,32,24]{1,2,0:T(8,128)S(1)} %get-tuple-element.5, f32[16,32,24]{1,2,0:T(8,128)S(1)} %get-tuple-element.4), kind=kOutput, calls=%fused_computation.5 | convolution fusion | flops 3035144192 | bytes 57860096 | tf_op jit(solution)/shard_map/rjf,rjp->rfp/dot_general | solution.py:68
  (24 shorter events, 0.3 us)
Async XLA Ops:
  7.2 436.1 %all-gather.2.cloned.1.call-start = ((), (), s32[]{:S(2)}) async-start(), calls=%async_computation.2 | async-start | bytes 2949120 | tf_op jit(solution)/shard_map/all_gather | solution.py:49
  11.4 381.8 %slice-start = ((s8[15925248]{0:T(1024)(128)(4,1)}), s8[4194304]{0:T(1024)(128)(4,1)S(1)}, s32[]{:S(2)}) async-start(s8[15925248]{0:T(1024)(128)(4,1)} %bitcast.29), calls=%async_computation.3 | async-start | bytes 8388608
  13.3 379.8 %slice-start.1 = ((s8[15925248]{0:T(1024)(128)(4,1)}), s8[4194304]{0:T(1024)(128)(4,1)S(1)}, s32[]{:S(2)}) async-start(s8[15925248]{0:T(1024)(128)(4,1)} %bitcast.29), calls=%async_computation.4 | async-start | bytes 8388608
  13.3 379.9 %slice-start.2 = ((s8[15925248]{0:T(1024)(128)(4,1)}), s8[4194304]{0:T(1024)(128)(4,1)S(1)}, s32[]{:S(2)}) async-start(s8[15925248]{0:T(1024)(128)(4,1)} %bitcast.29), calls=%async_computation.5 | async-start | bytes 8388608
  13.3 379.9 %slice-start.3 = ((s8[15925248]{0:T(1024)(128)(4,1)}), s8[3342336]{0:T(1024)(128)(4,1)S(1)}, s32[]{:S(2)}) async-start(s8[15925248]{0:T(1024)(128)(4,1)} %bitcast.29), calls=%async_computation.6 | async-start | bytes 6684672
  393.2 45.8 %copy-start = (s32[32]{0:T(128)S(1)}, s32[32]{0:T(128)}, u32[]{:S(2)}) copy-start(s32[32]{0:T(128)} %param.7) | copy-start | bytes 388
  393.2 46.0 %copy-start.1 = (f32[24]{0:T(128)S(1)}, f32[24]{0:T(128)}, u32[]{:S(2)}) copy-start(f32[24]{0:T(128)} %param.9) | copy-start | bytes 292
  434.8 8.2 %all-to-all-start = ((bf16[4,2,3072]{2,1,0:T(2,128)(2,1)}), bf16[4,2,3072]{2,1,0:T(2,128)(2,1)S(1)}, u32[]{:S(2)}, u32[]{:S(2)}) async-start(bf16[4,2,3072]{2,1,0:T(2,128)(2,1)} %reshape.176), calls=%async_computation | async-start | bytes 98304 | tf_op jit(solution)/shard_map/all_to_all | solution.py:48
  455.2 7.6 %all-to-all-start.1 = ((bf16[4,2,3072]{2,1,0:T(2,128)(2,1)}), bf16[4,2,3072]{2,1,0:T(2,128)(2,1)S(1)}, u32[]{:S(2)}, u32[]{:S(2)}) async-start(bf16[4,2,3072]{2,1,0:T(2,128)(2,1)} %reshape.178), calls=%async_computation.1 | async-start | bytes 98304 | tf_op jit(solution)/shard_map/all_to_all | solution.py:58
Sparse Core Ops, SparseCore 0:
  10.2 57.3 all-gather.1
where the time goes:
time: 501 us; the launch traced here: 499 us
  other arithmetic  389 us (78%)
  matrix products  75.5 us (15%)
  between operations  14.6 us (3%)
  starting transfers between devices  7.81 us (2%)
  local copies, waits for them, and re-layouts  7.52 us (2%)
    select_n x1, other arithmetic, cycle_tables(): cosine = jnp.where(live, jnp.cos(theta), jnp.float32(0.0))  380 us
    dot_general x1, matrix products, per_device(): coeffs = jnp.einsum('rfp,rjp->rfj', grid_field, tables, precision=highest)  40.3 us
    dot_general x1, matrix products, per_device(): grid_out = jnp.einsum('rjf,rjp->rfp', stacked, tables, precision=highest)  28.3 us
  transfers between devices with their start and end apart: 3, of which 2 were waited for; matrix products, arithmetic and copies ran while one was open for 86% of the time, Pallas kernels for 0%

commit v1 on v0

v1 whole, which is shorter than its diff:
```python
import functools
import math

import jax
import jax.numpy as jnp
from jax import lax
from jax.experimental import pallas as pl
from jax.experimental.pallas import tpu as pltpu
from jax.sharding import PartitionSpec as P

WIDTH = 256
GROUP = 14
SERIES = tuple((-1.0) ** i * (2.0 * math.pi) ** (2 * i + 1) / math.factorial(2 * i + 1) for i in range(6))


def quarter(shape, axis, waves, marks):
    place = lax.broadcasted_iota(jnp.int32, shape, axis)
    result = jnp.full(shape, marks[-1], jnp.float32)
    for i in range(len(marks) - 2, -1, -1):
        result = jnp.where(place < (i + 1) * waves, jnp.float32(marks[i]), result)
    return result


def wave_of(product, length, inverse, shift):
    rest = product - jnp.floor(product * inverse) * length
    turns = rest * inverse + shift
    turns = turns - jnp.round(turns)
    v = 0.25 - jnp.abs(turns)
    square = v * v
    total = jnp.full_like(v, SERIES[-1])
    for term in SERIES[-2::-1]:
        total = total * square + jnp.float32(term)
    return total * v


def halves(value):
    high = value.astype(jnp.bfloat16)
    return high, (value - high.astype(jnp.float32)).astype(jnp.bfloat16)


def phases(lane_waves, chunks, length, inverse, shift):
    index = lax.broadcasted_iota(jnp.int32, (chunks, lane_waves.shape[1]), 0).astype(jnp.float32)
    return wave_of(lane_waves * (index * float(WIDTH)), length, inverse, shift)


def forward_kernel(waves, start, lengths, lane_waves_ref, *refs):
    x_refs, (out_ref, tail_ref) = refs[:-2], refs[-2:]
    fields, points = out_ref.shape[1], x_refs[0].shape[2]
    rows = tail_ref.shape[0]
    full = points // WIDTH
    chunks = -(-(full + 1) // GROUP) * GROUP
    whole = lengths[pl.program_id(0) + start]
    length = whole.astype(jnp.float32)
    inverse = 1.0 / jnp.full((1, 4 * waves), length, jnp.float32)
    lane_waves = lane_waves_ref[...]
    step = lax.broadcasted_iota(jnp.int32, (WIDTH, 4 * waves), 0).astype(jnp.float32)
    table = wave_of(
        lane_waves * step, length, inverse, quarter((1, 4 * waves), 1, waves, (0.0, 0.25, 0.25, 0.0))
    )
    table_high, table_low = halves(table)
    both = jnp.concatenate([table_high, table_low], axis=1)
    turn = phases(
        lane_waves, chunks, length, inverse, quarter((1, 4 * waves), 1, waves, (0.0, 0.0, -0.25, 0.25))
    )
    tail_ref[...] = jnp.zeros_like(tail_ref)
    if points > full * WIDTH:
        for i, x_ref in enumerate(x_refs):
            block = x_ref.shape[1]
            tail_ref[i * block : (i + 1) * block, : points - full * WIDTH] = x_ref[0, :, full * WIDTH :]
    column = lax.broadcasted_iota(jnp.int32, (1, WIDTH), 1)
    total = jnp.zeros((rows, 4 * waves), jnp.float32)
    for first in range(0, chunks, GROUP):
        parts = []
        for c in range(first, first + GROUP):
            if c > full:
                parts.append(jnp.zeros((rows, WIDTH), jnp.float32))
                continue
            if c == full:
                part = tail_ref[...]
            else:
                part = jnp.concatenate([x_ref[0, :, c * WIDTH : (c + 1) * WIDTH] for x_ref in x_refs], axis=0)
                if rows > fields:
                    part = jnp.concatenate([part, jnp.zeros((rows - fields, WIDTH), jnp.float32)], axis=0)
            parts.append(jnp.where(column + c * WIDTH < whole, part, 0.0))
        high, low = halves(jnp.concatenate(parts, axis=0))
        wide = jnp.dot(high, both, preferred_element_type=jnp.float32)
        rest = jnp.dot(low, table_high, preferred_element_type=jnp.float32)
        found = wide[:, : 4 * waves] + wide[:, 4 * waves :] + rest
        for c in range(GROUP):
            if first + c <= full:
                total = total + found[c * rows : (c + 1) * rows] * turn[first + c : first + c + 1]
    total = total + pltpu.roll(total, 2 * waves, 1)
    alive = 2.0 * lane_waves < length
    total = jnp.where(alive, total * lax.rsqrt(jnp.full((1, 4 * waves), length, jnp.float32)), 0.0)
    out_ref[0] = total[:fields, : 2 * waves].astype(jnp.bfloat16)


def inverse_kernel(waves, split, lengths, lane_waves_ref, row_waves_ref, b_ref, grid_ref, held_ref, sems):
    fields, points = grid_ref.shape[1], grid_ref.shape[2]
    slots = held_ref.shape[0]
    now, cycles = pl.program_id(0), pl.num_programs(0)
    slot = lax.rem(now, slots)
    block = fields // split

    def copies(step):
        at = lax.rem(step, slots)
        return [
            pltpu.make_async_copy(
                held_ref.at[at, pl.ds(r * block, block), :],
                grid_ref.at[step, pl.ds(r * block, block), :],
                sems.at[at, r],
            )
            for r in range(split)
        ]

    @pl.when(now >= slots)
    def _():
        for copy in copies(now - slots):
            copy.wait()

    rows = b_ref.shape[1]
    full = points // WIDTH
    chunks = -(-(full + 1) // GROUP) * GROUP
    whole = lengths[pl.program_id(0)]
    length = whole.astype(jnp.float32)
    inverse = 1.0 / jnp.full((1, 4 * waves), length, jnp.float32)
    lane_waves = lane_waves_ref[...]
    step = lax.broadcasted_iota(jnp.int32, (4 * waves, WIDTH), 1).astype(jnp.float32)
    table = wave_of(
        row_waves_ref[...] * step,
        length,
        1.0 / jnp.full((1, WIDTH), length, jnp.float32),
        quarter((4 * waves, 1), 0, waves, (0.0, 0.25, 0.0, 0.25)),
    )
    both = jnp.concatenate(halves(table), axis=0)
    turn = phases(
        lane_waves, chunks, length, inverse, quarter((1, 4 * waves), 1, waves, (0.0, 0.0, 0.25, -0.25))
    )
    scale = jnp.where(lane_waves == 0.0, 1.0, 2.0) * lax.rsqrt(jnp.full((1, 4 * waves), float(waves), jnp.float32))
    scale = jnp.where(2.0 * lane_waves < length, scale, 0.0)
    coeffs = b_ref[0].astype(jnp.float32) * scale
    column = lax.broadcasted_iota(jnp.int32, (1, WIDTH), 1)
    for first in range(0, chunks, GROUP):
        parts = [coeffs * turn[c : c + 1] for c in range(first, first + GROUP)]
        high = jnp.concatenate(parts, axis=0).astype(jnp.bfloat16)
        value = jnp.dot(
            jnp.concatenate([high, high], axis=1), both, preferred_element_type=jnp.float32
        )
        for c in range(first, first + GROUP):
            if c > full:
                continue
            part = value[(c - first) * rows : (c - first) * rows + fields]
            part = jnp.where(column + c * WIDTH < whole, part, 0.0)
            if c < full:
                held_ref[slot, :, c * WIDTH : (c + 1) * WIDTH] = part
            elif points > full * WIDTH:
                held_ref[slot, :, full * WIDTH :] = part[:, : points - full * WIDTH]
    for copy in copies(now):
        copy.start()

    @pl.when(now == cycles - 1)
    def _():
        for back in range(min(slots, grid_ref.shape[0]) - 1, -1, -1):
            for copy in copies(now - back):
                copy.wait()


def forward(grid_field, cycle_points, wave_ids, start, cycles):
    fields, points = grid_field.shape[1:]
    waves = wave_ids.shape[0]
    rows = -(-fields // 8) * 8
    split = 1
    lane_waves = jnp.tile(wave_ids.astype(jnp.float32), 4)[None, :]
    return pl.pallas_call(
        functools.partial(forward_kernel, waves, start),
        grid_spec=pltpu.PrefetchScalarGridSpec(
            num_scalar_prefetch=1,
            grid=(cycles,),
            in_specs=[
                pl.BlockSpec((1, 4 * waves), lambda i, s: (0, 0)),
            ]
            + [
                pl.BlockSpec((1, fields // split, points), functools.partial(lambda r, i, s: (i + start, r, 0), r))
                for r in range(split)
            ],
            out_specs=pl.BlockSpec((1, fields, 2 * waves), lambda i, s: (i, 0, 0)),
            scratch_shapes=[pltpu.VMEM((rows, WIDTH), jnp.float32)],
        ),
        out_shape=jax.ShapeDtypeStruct((cycles, fields, 2 * waves), jnp.bfloat16),
        compiler_params=pltpu.CompilerParams(vmem_limit_bytes=32 * 2**20),
        cost_estimate=pl.CostEstimate(
            flops=4 * cycles * fields * points * 4 * waves,
            bytes_accessed=4 * cycles * fields * points,
            transcendentals=0,
        ),
    )(cycle_points, lane_waves, *[grid_field] * split)


def inverse(coeffs, cycle_points, wave_ids, fields, points):
    cycles, rows, lanes = coeffs.shape
    split = rows // 8 if rows == fields else 1
    waves = wave_ids.shape[0]
    plain = wave_ids.astype(jnp.float32)
    lane_waves = jnp.tile(plain, 4)[None, :]
    row_waves = jnp.tile(plain, 4)[:, None]
    return pl.pallas_call(
        functools.partial(inverse_kernel, waves, split),
        grid_spec=pltpu.PrefetchScalarGridSpec(
            num_scalar_prefetch=1,
            grid=(cycles,),
            in_specs=[
                pl.BlockSpec((1, 4 * waves), lambda i, s: (0, 0)),
                pl.BlockSpec((4 * waves, 1), lambda i, s: (0, 0)),
                pl.BlockSpec((1, rows, lanes), lambda i, s: (i, 0, 0)),
            ],
            out_specs=pl.BlockSpec(memory_space=pl.ANY),
            scratch_shapes=[
                pltpu.VMEM((4, fields, points), jnp.float32),
                pltpu.SemaphoreType.DMA((4, split)),
            ],
        ),
        out_shape=jax.ShapeDtypeStruct((cycles, fields, points), jnp.float32),
        compiler_params=pltpu.CompilerParams(vmem_limit_bytes=56 * 2**20),
        cost_estimate=pl.CostEstimate(
            flops=4 * cycles * fields * points * 4 * waves,
            bytes_accessed=4 * cycles * fields * points,
            transcendentals=0,
        ),
    )(cycle_points, lane_waves, row_waves, coeffs)


def legendre_kernel(waves_ref, f_ref, table_ref, factor_ref, spectra_ref, back_ref):
    table = table_ref[0]
    size = f_ref.shape[2]
    cut_off = table.shape[1]
    degree = lax.broadcasted_iota(jnp.int32, (1, cut_off), 1)
    keep = degree >= waves_ref[pl.program_id(0)]
    spectral = lax.dot_general(
        f_ref[0], table, (((0,), (0,)), ((), ())), preferred_element_type=jnp.float32
    )
    spectra = jnp.where(keep, spectral, 0.0).astype(jnp.bfloat16)
    wide = spectra.astype(jnp.float32)
    damped = (wide * factor_ref[...]).astype(jnp.bfloat16)
    back_ref[0] = lax.dot_general(
        table, damped, (((1,), (1,)), ((), ())), preferred_element_type=jnp.float32
    ).astype(jnp.bfloat16)
    spectra_ref[0] = spectra.reshape(spectra_ref.shape[1:])


def legendre_pair(own_waves, fourier, table, factor):
    per_group, cycles, size = fourier.shape
    cut_off = table.shape[2]
    return pl.pallas_call(
        legendre_kernel,
        grid_spec=pltpu.PrefetchScalarGridSpec(
            num_scalar_prefetch=1,
            grid=(per_group,),
            in_specs=[
                pl.BlockSpec((1, cycles, size), lambda i, s: (i, 0, 0)),
                pl.BlockSpec((1, cycles, cut_off), lambda i, s: (i, 0, 0)),
                pl.BlockSpec((size, cut_off), lambda i, s: (0, 0)),
            ],
            out_specs=[
                pl.BlockSpec((1, size // 2, 2, cut_off), lambda i, s: (i, 0, 0, 0)),
                pl.BlockSpec((1, cycles, size), lambda i, s: (i, 0, 0)),
            ],
        ),
        out_shape=[
            jax.ShapeDtypeStruct((per_group, size // 2, 2, cut_off), jnp.bfloat16),
            jax.ShapeDtypeStruct((per_group, cycles, size), jnp.bfloat16),
        ],
        compiler_params=pltpu.CompilerParams(vmem_limit_bytes=56 * 2**20),
        cost_estimate=pl.CostEstimate(
            flops=4 * per_group * cycles * size * cut_off,
            bytes_accessed=2 * per_group * (cycles + size) * cut_off,
            transcendentals=0,
        ),
    )(own_waves, fourier, table, factor)


def damping_factor(diffusion, cut_off):
    degree = jnp.arange(cut_off, dtype=jnp.int32).astype(jnp.float32)
    ratio = degree * (degree + 1.0) / jnp.float32(cut_off * (cut_off - 1))
    return 1.0 / (1.0 + diffusion[:, None] * (ratio * ratio)[None, :])


def ring_gather(legendre, held):
    n = lax.axis_size("ba")
    me = lax.axis_index("ba")
    per_group, share, cut_off = legendre.shape
    ring = list(range(0, n, 2)) + list(range(1, n, 2))[::-1]
    evens = (n + 1) // 2
    mine = jnp.where(me % 2 == 0, me // 2, n - 1 - me // 2)
    ahead = [(ring[i], ring[(i + 1) % n]) for i in range(n)]
    behind = [(ring[i], ring[(i - 1) % n]) for i in range(n)]

    def put(total, shard, first, hop):
        at = lax.rem(mine + hop + 2 * n, n)
        source = jnp.where(at < evens, 2 * at, 2 * (n - 1 - at) + 1)
        return lax.dynamic_update_slice(total, shard, (first, source * share, 0))

    total = jnp.zeros((per_group, n * share, cut_off), legendre.dtype)
    total = put(total, legendre, 0, 0)
    up = down = legendre
    half = per_group // 2
    for hop in range(1, n // 2 + 1):
        if 2 * hop == n:
            up, down = up[:half], down[half:]
        up = lax.ppermute(up, "ba", ahead)
        down = lax.ppermute(down, "ba", behind)
        if hop == 1:
            up, down, held = lax.optimization_barrier((up, down, held))
        total = put(total, up, 0, -hop)
        total = put(total, down, half if 2 * hop == n else 0, hop)
    return total, held


def per_device(grid_field, cycle_points, wave_ids, legendre, diffusion):
    groups = lax.axis_size("aa")
    waves_total = wave_ids.shape[0]
    per_group = waves_total // groups
    cycle_count, local_fields, points = grid_field.shape
    cut_off = legendre.shape[2]
    own_waves = lax.dynamic_slice_in_dim(wave_ids, lax.axis_index("aa") * per_group, per_group)
    factor = jnp.repeat(damping_factor(diffusion, cut_off), 2, axis=0)
    fourier = forward(grid_field, cycle_points, wave_ids, 0, cycle_count)
    table_all, fourier = ring_gather(legendre, fourier)
    fourier = fourier.reshape(cycle_count, local_fields, 2, waves_total)
    by_wave = jnp.transpose(fourier, (3, 0, 1, 2)).reshape(
        waves_total, cycle_count, local_fields * 2
    )
    gathered = lax.all_to_all(by_wave, "aa", split_axis=0, concat_axis=1, tiled=True)
    spectra, returned = legendre_pair(own_waves, gathered, table_all, factor)
    by_band = lax.all_to_all(returned, "aa", split_axis=1, concat_axis=0, tiled=True)
    pairs = jnp.transpose(
        by_band.reshape(waves_total, cycle_count, local_fields, 2), (1, 2, 3, 0)
    )
    real, imag = pairs[:, :, 0], pairs[:, :, 1]
    coeffs = jnp.concatenate([real, imag, imag, real], axis=2)
    rows = -(-local_fields // 8) * 8
    if rows > local_fields:
        coeffs = jnp.pad(coeffs, ((0, 0), (0, rows - local_fields), (0, 0)))
    grid_out = inverse(coeffs, cycle_points, wave_ids, local_fields, points)
    return (spectra, grid_out)


def solution(mesh):
    in_specs = (P("aa", "ba", None), P("aa"), P(), P("aa", "ba", None), P("ba"))
    out_specs = (P("aa", "ba", None, None), P("aa", "ba", None))
    return jax.shard_map(
        per_device, mesh=mesh, in_specs=in_specs, out_specs=out_specs, check_vma=False
    )
```

time: 501 us -> 92 us (0.18)
  other arithmetic: 389 us -> 2.22 us
  matrix products: 75.5 us -> 0 us
  Pallas kernels: 0 us -> 30.5 us
  waiting for transfers between devices: 4.76 us -> 21.4 us
  between operations: 14.6 us -> 0.83 us
  local copies, waits for them, and re-layouts: 7.52 us -> 19.8 us
  starting transfers between devices: 7.81 us -> 15.9 us
    select_n x2 -> x0, other arithmetic: 380 us -> none  [the longest x1 380 us: cycle_tables(): cosine = jnp.where(live, jnp.cos(theta), jnp.float32(0.0))]
    dot_general x4 -> x0, matrix products: 75.5 us -> none  [the longest x1 40.3 us: per_device(): coeffs = jnp.einsum('rfp,rjp->rfj', grid_field, tables, precision=highest)]
    pallas_call x0 -> x3, Pallas kernels: none -> 30.5 us  [the longest x1 12.2 us: inverse(): pl.pallas_call(functools.partial(inverse_kernel, waves, split), grid_spec...]
    ppermute x0 -> x8, waiting for transfers between devices: none -> 17.2 us  [the longest x4 15.5 us: ring_gather(): up = lax.ppermute(up, 'ba', ahead)]
    ppermute x0 -> x8, starting transfers between devices: none -> 9.32 us  [the longest x4 8.69 us: ring_gather(): up = lax.ppermute(up, 'ba', ahead)]
    unnamed x16, local copies, waits for them, and re-layouts: 1.96 us -> 11.1 us
  transfers between devices with their start and end apart: 3 -> 10, of which waited for: 2 -> 6; matrix products, arithmetic and copies ran while one was open for 86% -> 9% of each run, Pallas kernels for 0% -> 11%
where the time goes in v1:
time: 92 us; the launch traced here: 90.7 us
  Pallas kernels  30.5 us (33%)
  waiting for transfers between devices  21.4 us (23%)
  local copies, waits for them, and re-layouts  19.8 us (22%)
  starting transfers between devices  15.9 us (17%)
  other arithmetic  2.22 us (2%)
    ppermute x4, waiting for transfers between devices, ring_gather(): up = lax.ppermute(up, 'ba', ahead)  15.5 us
    pallas_call x1, Pallas kernels, inverse(): pl.pallas_call(functools.partial(inverse_kernel, waves, split), grid_spec...  12.2 us
    unnamed x16, local copies, waits for them, and re-layouts  11.1 us
    pallas_call x1, Pallas kernels, forward(): pl.pallas_call(functools.partial(forward_kernel, waves, start), grid_spec...  10.4 us
    ppermute x4, starting transfers between devices, ring_gather(): up = lax.ppermute(up, 'ba', ahead)  8.69 us
    pallas_call x1, Pallas kernels, legendre_pair(): pl.pallas_call(legendre_kernel, grid_spec=pltpu.PrefetchScalarGridSpec(nu...  7.97 us
    all_to_all x1, starting transfers between devices, per_device(): lax.all_to_all(returned, 'aa', split_axis=1, concat_axis=0, tiled=True)  3.27 us
    all_to_all x1, waiting for transfers between devices, per_device(): lax.all_to_all(returned, 'aa', split_axis=1, concat_axis=0, tiled=True)  3.27 us
  transfers between devices with their start and end apart: 10, of which 6 were waited for; matrix products, arithmetic and copies ran while one was open for 9% of the time, Pallas kernels for 11%

profile of v1, /device:TPU:0, one launch (start us, length us, event | category | flops | bytes accessed | tf_op | source)
XLA Modules:
  0.0 90.7 jit_solution(7429733654561568659)
XLA Ops:
  0.6 3.1 %collective-permute-start = (bf16[8,8,2560]{2,1,0:T(8,128)(2,1)}, bf16[8,8,2560]{2,1,0:T(8,128)(2,1)S(1)}, u32[]{:S(2)}, u32[]{:S(2)}) collective-permute-start(bf16[8,8,2560]{2,1,0:T(8,128)(2,1)} %param.8), channel_id=1, source_target_pairs={{0,2},{2,4},{4,6},{6,7},{7,5},{5,3},{3,1},{1,0},{8,10},{10,12},{12... | collective-permute-start | bytes 983048 | tf_op jit(solution)/shard_map/ppermute | solution.py:309
  3.7 0.7 convert_element_type.11
  4.4 1.3 %dynamic_slice.3.waves_ref = s32[8]{0:T(128)} dynamic-slice(s32[32]{0:T(128)} %param.7, s32[]{:T(128)S(6)} %select_n.72), dynamic_slice_sizes={8} | dynamic-slice | bytes 68 | tf_op jit(solution)/shard_map/dynamic_slice | solution.py:324
  5.8 0.8 add_divide_fusion
  6.7 1.1 %reshape.29.factor_ref = f32[48,2560]{1,0:T(8,128)} reshape(f32[24,2,2560]{2,1,0:T(2,128)S(1)} %broadcast_in_dim.9) | data formatting | bytes 983040 | tf_op jit(solution)/shard_map/reshape | solution.py:325
  7.9 5.5 %copy-done = f32[16,24,10256]{2,1,0:T(8,128)S(1)} copy-done((f32[16,24,10256]{2,1,0:T(8,128)S(1)}, f32[16,24,10256]{2,1,0:T(8,128)}, u32[]{:S(2)}) %copy-start) | copy-done | bytes 15753240
  13.4 0.7 copy-done.2
  14.0 10.4 %shard_map.68 = bf16[16,24,64]{2,1,0:T(8,128)(2,1)S(1)} custom-call(s32[16]{0:T(128)S(1)} %copy-done.2, f32[1,128]{1,0:T(1,128)S(1)} %broadcast_in_dim_tile.7.lane_waves_ref, f32[16,24,10256]{2,1,0:T(8,128)S(1)} %copy-done), custom_call_target="tpu_custom_call" | custom-call | flops 2016411648 | bytes 15753216 | tf_op jit(solution)/shard_map/pallas_call | solution.py:174
  24.6 0.7 copy-done.4
  25.4 0.7 copy-done.5
  26.6 0.8 reshape.31
  27.4 3.3 %all-to-all-start = ((bf16[4,2,3072]{2,1,0:T(2,128)(2,1)}), bf16[4,2,3072]{2,1,0:T(2,128)(2,1)S(1)}, u32[]{:S(2)}, u32[]{:S(2)}) async-start(bf16[4,2,3072]{2,1,0:T(2,128)(2,1)} %reshape.31), calls=%async_computation | async-start | bytes 98304 | tf_op jit(solution)/shard_map/all_to_all | solution.py:332
  30.7 2.1 %collective-permute-start.2 = (bf16[8,8,2560]{2,1,0:T(8,128)(2,1)}, bf16[8,8,2560]{2,1,0:T(8,128)(2,1)}, u32[]{:S(2)}, u32[]{:S(2)}) collective-permute-start(bf16[8,8,2560]{2,1,0:T(8,128)(2,1)} %copy-done.5), channel_id=1, source_target_pairs={{0,2},{2,4},{4,6},{6,7},{7,5},{5,3},{3,1},{1,0},{8,10},{10,12},{12... | collective-permute-start | bytes 983048 | tf_op jit(solution)/shard_map/ppermute | solution.py:309
  32.8 1.0 %constant_dynamic-update-slice_fusion.7 = bf16[8,64,2560]{2,1,0:T(8,128)(2,1)S(1)} fusion(bf16[8,64,2560]{2,1,0:T(8,128)(2,1)S(1)} %constant_dynamic-update-slice_fusion.8, bf16[8,8,2560]{2,1,0:T(8,128)(2,1)} %copy-done.5, s32[]{:T(128)S(6)} %select_n.79), kind=kLoop, calls=%fused_computation.14 | loop fusion | bytes 655364 | tf_op jit(solution)/shard_map/dynamic_update_slice | solution.py:300
  33.8 0.9 all-to-all-done
  34.9 0.7 copy.21
  35.5 5.8 %collective-permute-done.2 = bf16[8,8,2560]{2,1,0:T(8,128)(2,1)} collective-permute-done((bf16[8,8,2560]{2,1,0:T(8,128)(2,1)}, bf16[8,8,2560]{2,1,0:T(8,128)(2,1)}, u32[]{:S(2)}, u32[]{:S(2)}) %collective-permute-start.2) | collective-permute-done | bytes 327712 | tf_op jit(solution)/shard_map/ppermute | solution.py:309
  41.3 1.8 %collective-permute-start.4 = (bf16[8,8,2560]{2,1,0:T(8,128)(2,1)}, bf16[8,8,2560]{2,1,0:T(8,128)(2,1)S(1)}, u32[]{:S(2)}, u32[]{:S(2)}) collective-permute-start(bf16[8,8,2560]{2,1,0:T(8,128)(2,1)} %collective-permute-done.2), channel_id=1, source_target_pairs={{0,2},{2,4},{4,6},{6,7},{7,5},{5,3},{3,1},{1,0},{8,10},{10,12},{12... | collective-permute-start | bytes 983048 | tf_op jit(solution)/shard_map/ppermute | solution.py:309
  43.3 1.0 %constant_dynamic-update-slice_fusion.5 = bf16[8,64,2560]{2,1,0:T(8,128)(2,1)S(1)} fusion(bf16[8,64,2560]{2,1,0:T(8,128)(2,1)S(1)} %constant_dynamic-update-slice_fusion.6, bf16[8,8,2560]{2,1,0:T(8,128)(2,1)} %collective-permute-done.2, s32[]{:T(128)S(6)} %select_n.83), kind=kLoop, calls=%fused_computation.12 | loop fusion | bytes 655364 | tf_op jit(solution)/shard_map/dynamic_update_slice | solution.py:300
  44.4 6.5 %collective-permute-done.4 = bf16[8,8,2560]{2,1,0:T(8,128)(2,1)S(1)} collective-permute-done((bf16[8,8,2560]{2,1,0:T(8,128)(2,1)}, bf16[8,8,2560]{2,1,0:T(8,128)(2,1)S(1)}, u32[]{:S(2)}, u32[]{:S(2)}) %collective-permute-start.4) | collective-permute-done | bytes 327712 | tf_op jit(solution)/shard_map/ppermute | solution.py:309
  50.9 1.7 %collective-permute-start.6 = (bf16[4,8,2560]{2,1,0:T(8,128)(2,1)S(1)}, bf16[4,8,2560]{2,1,0:T(8,128)(2,1)S(1)}, u32[]{:S(2)}, u32[]{:S(2)}) collective-permute-start(bf16[4,8,2560]{2,1,0:T(8,128)(2,1)S(1)} %slice.16), channel_id=1, source_target_pairs={{0,2},{2,4},{4,6},{6,7},{7,5},{5,3},{3,1},{1,0},{8,10},{10,12},{12... | collective-permute-start | bytes 491528 | tf_op jit(solution)/shard_map/ppermute | solution.py:309
  53.1 3.2 %collective-permute-done.6 = bf16[4,8,2560]{2,1,0:T(8,128)(2,1)S(1)} collective-permute-done((bf16[4,8,2560]{2,1,0:T(8,128)(2,1)S(1)}, bf16[4,8,2560]{2,1,0:T(8,128)(2,1)S(1)}, u32[]{:S(2)}, u32[]{:S(2)}) %collective-permute-start.6) | collective-permute-done | bytes 163872 | tf_op jit(solution)/shard_map/ppermute | solution.py:309
  56.3 1.7 %collective-permute-done.7 = bf16[4,8,2560]{2,1,0:T(8,128)(2,1)S(1)} collective-permute-done((bf16[4,8,2560]{2,1,0:T(8,128)(2,1)S(1)}, bf16[4,8,2560]{2,1,0:T(8,128)(2,1)S(1)}, u32[]{:S(2)}, u32[]{:S(2)}) %collective-permute-start.7) | collective-permute-done | bytes 163872 | tf_op jit(solution)/shard_map/ppermute | solution.py:310
  58.1 1.5 %copy-done.3 = bf16[8,64,2560]{2,1,0:T(8,128)(2,1)} copy-done((bf16[8,64,2560]{2,1,0:T(8,128)(2,1)}, bf16[8,64,2560]{2,1,0:T(8,128)(2,1)S(1)}, u32[]{:S(2)}) %copy-start.3) | copy-done | bytes 2621464
  59.6 8.0 %shard_map.69 = (bf16[8,24,2,2560]{3,2,1,0:T(2,128)(2,1)}, bf16[8,64,48]{2,1,0:T(8,128)(2,1)}) custom-call(s32[8]{0:T(128)} %dynamic_slice.3.waves_ref, bf16[8,64,48]{2,1,0:T(8,128)(2,1)} %bitcast.26, bf16[8,64,2560]{2,1,0:T(8,128)(2,1)} %copy-done.3, f32[48,2560]{1,0:T(8,128)} %reshape.29.factor_ref), custom_call_target="tpu_custom_call" | custom-call | flops 251658240 | bytes 4587520 | tf_op jit(solution)/shard_map/pallas_call | solution.py:253
  67.5 1.0 %copy.27 = bf16[8,64,48]{2,0,1:T(8,128)(2,1)S(1)} copy(bf16[8,64,48]{2,1,0:T(8,128)(2,1)} %get-tuple-element.11) | data formatting | bytes 98304 | tf_op jit(solution)/shard_map/pallas_call | solution.py:253
  68.5 0.8 reshape.33
  69.3 3.3 %all-to-all-start.1 = ((bf16[4,2,3072]{2,1,0:T(2,128)(2,1)}), bf16[4,2,3072]{2,1,0:T(2,128)(2,1)S(1)}, u32[]{:S(2)}, u32[]{:S(2)}) async-start(bf16[4,2,3072]{2,1,0:T(2,128)(2,1)} %reshape.33), calls=%async_computation.1 | async-start | bytes 98304 | tf_op jit(solution)/shard_map/all_to_all | solution.py:334
  72.6 0.7 broadcast_in_dim_tile.9.row_waves_ref
  73.3 3.3 %all-to-all-done.1 = bf16[4,2,3072]{2,1,0:T(2,128)(2,1)S(1)} async-done(((bf16[4,2,3072]{2,1,0:T(2,128)(2,1)}), bf16[4,2,3072]{2,1,0:T(2,128)(2,1)S(1)}, u32[]{:S(2)}, u32[]{:S(2)}) %all-to-all-start.1) | async-done | bytes 49184 | tf_op jit(solution)/shard_map/all_to_all | solution.py:334
  77.7 0.8 pad_maximum_fusion.b_ref
  78.5 12.2 %shard_map.70 = f32[16,24,10256]{2,1,0:T(8,128)} custom-call(s32[16]{0:T(128)} %lengths.3, f32[1,128]{1,0:T(1,128)} %copy-done.1, f32[128,1]{1,0:T(8,128)} %broadcast_in_dim_tile.9.row_waves_ref, bf16[16,24,128]{2,1,0:T(8,128)(2,1)} %pad_maximum_fusion.b_ref), custom_call_target="tpu_custom_call" | custom-call | flops 2016411648 | bytes 15753216 | tf_op jit(solution)/shard_map/pallas_call | solution.py:206
  (37 shorter events, 2.9 us)
Async XLA Ops:
  0.6 24.8 %collective-permute-start = (bf16[8,8,2560]{2,1,0:T(8,128)(2,1)}, bf16[8,8,2560]{2,1,0:T(8,128)(2,1)S(1)}, u32[]{:S(2)}, u32[]{:S(2)}) collective-permute-start(bf16[8,8,2560]{2,1,0:T(8,128)(2,1)} %param.8), channel_id=1, source_target_pairs={{0,2},{2,4},{4,6},{6,7},{7,5},{5,3},{3,1},{1,0},{8,10},{10,12},{12... | collective-permute-start | bytes 983048 | tf_op jit(solution)/shard_map/ppermute | solution.py:309
  3.7 22.4 %collective-permute-start.1 = (bf16[8,8,2560]{2,1,0:T(8,128)(2,1)}, bf16[8,8,2560]{2,1,0:T(8,128)(2,1)S(1)}, u32[]{:S(2)}, u32[]{:S(2)}) collective-permute-start(bf16[8,8,2560]{2,1,0:T(8,128)(2,1)} %param.8), channel_id=1, source_target_pairs={{0,1},{2,0},{4,2},{6,4},{7,6},{5,7},{3,5},{1,3},{8,9},{10,8},{12,1... | collective-permute-start | bytes 983048 | tf_op jit(solution)/shard_map/ppermute | solution.py:310
  5.8 18.6 %copy-start.1 = (f32[1,128]{1,0:T(1,128)}, f32[1,128]{1,0:T(1,128)S(1)}, u32[]{:S(2)}) copy-start(f32[1,128]{1,0:T(1,128)S(1)} %broadcast_in_dim_tile.7.lane_waves_ref) | copy-start | bytes 1540
  7.9 5.5 %copy-start = (f32[16,24,10256]{2,1,0:T(8,128)S(1)}, f32[16,24,10256]{2,1,0:T(8,128)}, u32[]{:S(2)}) copy-start(f32[16,24,10256]{2,1,0:T(8,128)} %refs_0_.1) | copy-start | bytes 47259652
  13.4 0.7 copy-start.2
  24.4 1.0 %copy-start.4 = (bf16[8,8,2560]{2,1,0:T(8,128)(2,1)S(1)}, bf16[8,8,2560]{2,1,0:T(8,128)(2,1)}, u32[]{:S(2)}) copy-start(bf16[8,8,2560]{2,1,0:T(8,128)(2,1)} %param.8) | copy-start | bytes 983044
  25.4 0.7 copy-start.5
  27.4 7.3 %all-to-all-start = ((bf16[4,2,3072]{2,1,0:T(2,128)(2,1)}), bf16[4,2,3072]{2,1,0:T(2,128)(2,1)S(1)}, u32[]{:S(2)}, u32[]{:S(2)}) async-start(bf16[4,2,3072]{2,1,0:T(2,128)(2,1)} %reshape.31), calls=%async_computation | async-start | bytes 98304 | tf_op jit(solution)/shard_map/all_to_all | solution.py:332
  30.7 10.6 %collective-permute-start.2 = (bf16[8,8,2560]{2,1,0:T(8,128)(2,1)}, bf16[8,8,2560]{2,1,0:T(8,128)(2,1)}, u32[]{:S(2)}, u32[]{:S(2)}) collective-permute-start(bf16[8,8,2560]{2,1,0:T(8,128)(2,1)} %copy-done.5), channel_id=1, source_target_pairs={{0,2},{2,4},{4,6},{6,7},{7,5},{5,3},{3,1},{1,0},{8,10},{10,12},{12... | collective-permute-start | bytes 983048 | tf_op jit(solution)/shard_map/ppermute | solution.py:309
  32.8 10.4 %collective-permute-start.3 = (bf16[8,8,2560]{2,1,0:T(8,128)(2,1)S(1)}, bf16[8,8,2560]{2,1,0:T(8,128)(2,1)S(1)}, u32[]{:S(2)}, u32[]{:S(2)}) collective-permute-start(bf16[8,8,2560]{2,1,0:T(8,128)(2,1)S(1)} %collective-permute-done.1), channel_id=1, source_target_pairs={{0,1},{2,0},{4,2},{6,4},{7,6},{5,7},{3,5},{1,3},{8,9},{10,8},{12,1... | collective-permute-start | bytes 983048 | tf_op jit(solution)/shard_map/ppermute | solution.py:310
  41.3 9.6 %collective-permute-start.4 = (bf16[8,8,2560]{2,1,0:T(8,128)(2,1)}, bf16[8,8,2560]{2,1,0:T(8,128)(2,1)S(1)}, u32[]{:S(2)}, u32[]{:S(2)}) collective-permute-start(bf16[8,8,2560]{2,1,0:T(8,128)(2,1)} %collective-permute-done.2), channel_id=1, source_target_pairs={{0,2},{2,4},{4,6},{6,7},{7,5},{5,3},{3,1},{1,0},{8,10},{10,12},{12... | collective-permute-start | bytes 983048 | tf_op jit(solution)/shard_map/ppermute | solution.py:309
  43.1 9.5 %collective-permute-start.5 = (bf16[8,8,2560]{2,1,0:T(8,128)(2,1)S(1)}, bf16[8,8,2560]{2,1,0:T(8,128)(2,1)S(1)}, u32[]{:S(2)}, u32[]{:S(2)}) collective-permute-start(bf16[8,8,2560]{2,1,0:T(8,128)(2,1)S(1)} %collective-permute-done.3), channel_id=1, source_target_pairs={{0,1},{2,0},{4,2},{6,4},{7,6},{5,7},{3,5},{1,3},{8,9},{10,8},{12,1... | collective-permute-start | bytes 983048 | tf_op jit(solution)/shard_map/ppermute | solution.py:310
  50.9 5.4 %collective-permute-start.6 = (bf16[4,8,2560]{2,1,0:T(8,128)(2,1)S(1)}, bf16[4,8,2560]{2,1,0:T(8,128)(2,1)S(1)}, u32[]{:S(2)}, u32[]{:S(2)}) collective-permute-start(bf16[4,8,2560]{2,1,0:T(8,128)(2,1)S(1)} %slice.16), channel_id=1, source_target_pairs={{0,2},{2,4},{4,6},{6,7},{7,5},{5,3},{3,1},{1,0},{8,10},{10,12},{12... | collective-permute-start | bytes 491528 | tf_op jit(solution)/shard_map/ppermute | solution.py:309
  52.7 5.4 %collective-permute-start.7 = (bf16[4,8,2560]{2,1,0:T(8,128)(2,1)S(1)}, bf16[4,8,2560]{2,1,0:T(8,128)(2,1)S(1)}, u32[]{:S(2)}, u32[]{:S(2)}) collective-permute-start(bf16[4,8,2560]{2,1,0:T(8,128)(2,1)S(1)} %slice.17), channel_id=1, source_target_pairs={{0,1},{2,0},{4,2},{6,4},{7,6},{5,7},{3,5},{1,3},{8,9},{10,8},{12,1... | collective-permute-start | bytes 491528 | tf_op jit(solution)/shard_map/ppermute | solution.py:310
  58.1 1.5 %copy-start.3 = (bf16[8,64,2560]{2,1,0:T(8,128)(2,1)}, bf16[8,64,2560]{2,1,0:T(8,128)(2,1)S(1)}, u32[]{:S(2)}) copy-start(bf16[8,64,2560]{2,1,0:T(8,128)(2,1)S(1)} %constant_dynamic-update-slice_fusion.table_ref) | copy-start | bytes 7864324
  69.3 7.3 %all-to-all-start.1 = ((bf16[4,2,3072]{2,1,0:T(2,128)(2,1)}), bf16[4,2,3072]{2,1,0:T(2,128)(2,1)S(1)}, u32[]{:S(2)}, u32[]{:S(2)}) async-start(bf16[4,2,3072]{2,1,0:T(2,128)(2,1)} %reshape.33), calls=%async_computation.1 | async-start | bytes 98304 | tf_op jit(solution)/shard_map/all_to_all | solution.py:334
